TPU v7x, 128 devices: a whole 4x4x4 slice. The times are simulated.
128 devices in a mesh: row: 16 (over z, y), col: 8 (over x, core).
Axes of the slice: x: 4, y: 4, z: 4, core: 2. Of those that a mesh axis runs over, the one named last changes fastest.
Arguments:
- matrix: bfloat16 [28672, 28672], P('row', 'col'), may hold values from -1.5 to 16, as said below
Outputs:
- factored: bfloat16 [28672, 28672], P('row', 'col')
Inputs may be any that keep to these rules, and one draw needn't show every extreme that they name: `matrix`: in logical order, diagonal entries lie between 12 and 16 and off-diagonal entries have magnitude at most 1.5.
All inputs are finite; a program needn't handle non-finite values.
Results may differ from a plain program's by a relative error of at most 0.0025.
The roundings to bfloat16 on the way count: a program that leaves them out, or rounds other values in their place, can miss the bound.
Values may be sent and summed in bfloat16 or wider, within the bound.
A program may use at most 192 MiB of HBM per device.

v0:
```python
import jax
import jax.numpy as jnp
from jax import lax
from jax.sharding import PartitionSpec as P

NB = 256
STEPS = 2


def broadcast(block, axis, owner):
    block = jnp.where(lax.axis_index(axis) == owner, block, jnp.zeros_like(block))
    return lax.psum(block, axis)


def factor_block(block):
    work = block.astype(jnp.float32)
    size = work.shape[0]
    positions = jnp.arange(size, dtype=jnp.int32)

    def eliminate(column, work):
        values = lax.dynamic_slice_in_dim(work, column, 1, 1)[:, 0]
        pivot_row = lax.dynamic_slice_in_dim(work, column, 1, 0)[0]
        pivot = jnp.sum(jnp.where(positions == column, pivot_row, 0.0))
        scaled = jnp.where(positions > column, values / pivot, 0.0)
        across = jnp.where(positions > column, pivot_row, 0.0)
        work = work - scaled[:, None] * across[None, :]
        kept = jnp.where(positions > column, scaled, values)
        return jnp.where(positions[None, :] == column, kept[:, None], work)

    return lax.fori_loop(0, size, eliminate, work)


def invert_upper(upper):
    size = upper.shape[0]
    positions = jnp.arange(size, dtype=jnp.int32)

    def substitute(count, inverse):
        index = size - 1 - count
        line = lax.dynamic_slice_in_dim(upper, index, 1, 0)[0]
        strict = jnp.where(positions > index, line, 0.0)
        pivot = jnp.sum(jnp.where(positions == index, line, 0.0))
        unit = jnp.where(positions == index, 1.0, 0.0).astype(jnp.float32)
        fresh = (unit - jnp.dot(strict, inverse, precision=lax.Precision.HIGHEST)) / pivot
        return jnp.where(positions[:, None] == index, fresh[None, :], inverse)

    return lax.fori_loop(0, size, substitute, jnp.zeros((size, size), jnp.float32))


def invert_lower(lower):
    size = lower.shape[0]
    positions = jnp.arange(size, dtype=jnp.int32)

    def substitute(index, inverse):
        line = lax.dynamic_slice_in_dim(lower, index, 1, 0)[0]
        strict = jnp.where(positions < index, line, 0.0)
        unit = jnp.where(positions == index, 1.0, 0.0).astype(jnp.float32)
        fresh = unit - jnp.dot(strict, inverse, precision=lax.Precision.HIGHEST)
        return jnp.where(positions[:, None] == index, fresh[None, :], inverse)

    return lax.fori_loop(0, size, substitute, jnp.zeros((size, size), jnp.float32))


def solve_left(upper_inverse, panel, keep_rows):
    solved = jnp.dot(panel.astype(jnp.float32), upper_inverse, precision=lax.Precision.HIGHEST)
    return jnp.where(keep_rows[:, None], solved, 0.0).astype(jnp.bfloat16)


def solve_top(lower_inverse, panel, keep_cols):
    solved = jnp.dot(lower_inverse, panel.astype(jnp.float32), precision=lax.Precision.HIGHEST)
    return jnp.where(keep_cols[None, :], solved, 0.0).astype(jnp.bfloat16)


def on_device(matrix):
    grid_rows = lax.axis_size("row")
    grid_cols = lax.axis_size("col")
    local_rows, local_cols = matrix.shape
    row_block = jnp.arange(local_rows, dtype=jnp.int32) // NB * grid_rows + lax.axis_index("row")
    col_block = jnp.arange(local_cols, dtype=jnp.int32) // NB * grid_cols + lax.axis_index("col")
    work = matrix
    for section in range(STEPS):
        root_row = section % grid_rows
        root_col = section % grid_cols
        row_start = section // grid_rows * NB
        col_start = section // grid_cols * NB
        own_diag = work[row_start : row_start + NB, col_start : col_start + NB]
        diag_block = broadcast(own_diag, ("row", "col"), root_row * grid_cols + root_col)
        packed = factor_block(diag_block)
        upper = jnp.triu(packed)
        lower = jnp.tril(packed, -1) + jnp.eye(NB, dtype=jnp.float32)
        upper_inverse = invert_upper(upper)
        lower_inverse = invert_lower(lower)
        column_panel = work[:, col_start : col_start + NB]
        row_panel = work[row_start : row_start + NB, :]
        keep_rows = row_block > section
        keep_cols = col_block > section
        left_panel = broadcast(solve_left(upper_inverse, column_panel, keep_rows), "col", root_col)
        top_panel = broadcast(solve_top(lower_inverse, row_panel, keep_cols), "row", root_row)
        update = jnp.dot(left_panel, top_panel, preferred_element_type=jnp.float32)
        updated = (work.astype(jnp.float32) - update).astype(jnp.bfloat16)
        in_col = (col_block == section)[None, :]
        in_row = (row_block == section)[:, None]
        left_wide = jnp.tile(left_panel, (1, local_cols // NB))
        top_tall = jnp.tile(top_panel, (local_rows // NB, 1))
        packed_tiles = jnp.tile(packed.astype(jnp.bfloat16), (local_rows // NB, local_cols // NB))
        updated = jnp.where(in_col & keep_rows[:, None], left_wide, updated)
        updated = jnp.where(in_row & keep_cols[None, :], top_tall, updated)
        work = jnp.where(in_row & in_col, packed_tiles, updated)
    return work


def solution(mesh):
    in_specs = (P("row", "col"),)
    out_specs = P("row", "col")
    return jax.shard_map(
        on_device, mesh=mesh, in_specs=in_specs, out_specs=out_specs, check_vma=False
    )
```

profile of v0, /device:TPU:4, one launch (start us, length us, event | category | flops | bytes accessed | tf_op | source)
XLA Modules:
  0.0 2431.0 jit_solution(8581559107379441175)
XLA Ops:
  6.5 1.6 slice_select_fusion.1
  8.3 145.4 %all-reduce.7.cloned.1.call-done = bf16[256,256]{1,0:T(8,128)(2,1)} async-done(((bf16[256,256]{1,0:T(8,128)(2,1)}), bf16[256,256]{1,0:T(8,128)(2,1)}) %all-reduce.7.cloned.1.call-update) | async-done | bytes 131088 | tf_op jit(solution)/shard_map/psum | solution.py:12
  153.7 1.0 copy.16
  154.7 411.8 %while.94 = (s32[]{:T(128)}, f32[256,256]{0,1:T(8,128)S(1)}, s32[]{:T(128)}) while((s32[]{:T(128)}, f32[256,256]{0,1:T(8,128)S(1)}, s32[]{:T(128)}) %tuple.229), condition=%wide.region_3.4_spmd.clone.clone, body=%wide.region_1.3_spmd.clone.clone.sunk | while | flops 198913 | bytes 1060173 | solution.py:30
  566.7 424.2 %while.97 = (s32[]{:T(128)}, f32[256,256]{1,0:T(8,128)S(1)}, f32[256,256]{1,0:T(8,128)S(1)}, s32[]{:T(128)}, s32[]{:T(128)}, /*index=5*/s32[]{:T(128)}, s32[]{:T(128)}) while((s32[]{:T(128)}, f32[256,256]{1,0:T(8,128)S(1)}, f32[256,256]{1,0:T(8,128)S(1)}, s32[]{:T(128)}, s32[]{:T(128)}, /*index=5*/s32[]{:T(128)}, ...), condition=%wide.region_9.10_spmd.clone.clone, body=%wide.region_7.9_spmd.clone.clone.sunk | while | flops 985606 | bytes 796326 | solution.py:46
  567.5 0.7 subtract_divide_fusion.4
  569.2 0.7 subtract_divide_fusion.4
  570.8 0.7 subtract_divide_fusion.4
  584.1 0.7 subtract_divide_fusion.4
  585.8 0.7 subtract_divide_fusion.4
  587.4 0.7 subtract_divide_fusion.4
  599.0 0.7 subtract_divide_fusion.4
  600.7 0.7 subtract_divide_fusion.4
  602.3 0.7 subtract_divide_fusion.4
  615.6 0.7 subtract_divide_fusion.4
  617.2 0.7 subtract_divide_fusion.4
  618.9 0.7 subtract_divide_fusion.4
  630.5 0.7 subtract_divide_fusion.4
  632.2 0.7 subtract_divide_fusion.4
  633.8 0.7 subtract_divide_fusion.4
  647.1 0.7 subtract_divide_fusion.4
  648.7 0.7 subtract_divide_fusion.4
  650.4 0.7 subtract_divide_fusion.4
  662.0 0.7 subtract_divide_fusion.4
  990.9 3.8 fusion.40
  994.7 106.3 %while.96 = (s32[]{:T(128)}, f32[256,256]{1,0:T(8,128)S(1)}, f32[256,256]{1,0:T(8,128)S(1)}, s32[]{:T(128)}, s32[]{:T(128)}) while((s32[]{:T(128)}, f32[256,256]{1,0:T(8,128)S(1)}, f32[256,256]{1,0:T(8,128)S(1)}, s32[]{:T(128)}, s32[]{:T(128)}) %tuple.235), condition=%wide.region_5.6_spmd.clone.clone, body=%wide.region_4.5_spmd.clone.clone.sunk | while | flops 984579 | bytes 796256 | solution.py:60
  1101.1 4.5 fusion.35
  1105.9 6.4 tile.24
  1112.3 14.2 copy.27
  1126.6 7.1 tile.28
  1133.6 18.1 copy.20
  1151.7 41.9 %all-reduce.9.cloned.1.call-done = bf16[256,3584]{1,0:T(8,128)(2,1)} async-done(((bf16[256,3584]{1,0:T(8,128)(2,1)}), bf16[256,3584]{1,0:T(8,128)(2,1)}) %all-reduce.9.cloned.1.call-update) | async-done | bytes 1835024 | tf_op jit(solution)/shard_map/psum | solution.py:12
  1193.6 21.3 and_select_fusion.4
  1215.0 4.6 copy-done.2
  1220.5 138.3 %all-reduce.13.cloned.1.call-done = bf16[256,256]{1,0:T(8,128)(2,1)} async-done(((bf16[256,256]{1,0:T(8,128)(2,1)}), bf16[256,256]{1,0:T(8,128)(2,1)}) %all-reduce.13.cloned.1.call-update) | async-done | bytes 131088 | tf_op jit(solution)/shard_map/psum | solution.py:12
  1358.8 1.0 copy.21
  1359.8 411.8 %while.95 = (s32[]{:T(128)}, f32[256,256]{0,1:T(8,128)S(1)}, s32[]{:T(128)}) while((s32[]{:T(128)}, f32[256,256]{0,1:T(8,128)S(1)}, s32[]{:T(128)}) %tuple.238), condition=%wide.region_14.15_spmd.clone.clone, body=%wide.region_12.14_spmd.clone.clone.sunk | while | flops 198913 | bytes 1060173 | solution.py:30
  1771.8 424.2 %while.99 = (s32[]{:T(128)}, f32[256,256]{1,0:T(8,128)S(1)}, f32[256,256]{1,0:T(8,128)S(1)}, s32[]{:T(128)}, s32[]{:T(128)}, /*index=5*/s32[]{:T(128)}, s32[]{:T(128)}) while((s32[]{:T(128)}, f32[256,256]{1,0:T(8,128)S(1)}, f32[256,256]{1,0:T(8,128)S(1)}, s32[]{:T(128)}, s32[]{:T(128)}, /*index=5*/s32[]{:T(128)}, ...), condition=%wide.region_20.21_spmd.clone.clone, body=%wide.region_18.20_spmd.clone.clone.sunk | while | flops 985606 | bytes 796326 | solution.py:46
  2196.0 3.0 fusion.38
  2199.1 106.3 %while.98 = (s32[]{:T(128)}, f32[256,256]{1,0:T(8,128)S(1)}, f32[256,256]{1,0:T(8,128)S(1)}, s32[]{:T(128)}, s32[]{:T(128)}) while((s32[]{:T(128)}, f32[256,256]{1,0:T(8,128)S(1)}, f32[256,256]{1,0:T(8,128)S(1)}, s32[]{:T(128)}, s32[]{:T(128)}) %tuple.244), condition=%wide.region_16.17_spmd.clone.clone, body=%wide.region_15.16_spmd.clone.clone.sunk | while | flops 984579 | bytes 796256 | solution.py:60
  2305.4 4.5 fusion.34
  2310.1 6.3 tile.60
  2316.5 14.2 copy.28
  2330.7 1.5 copy.25
  2332.2 5.9 tile.64
  2338.0 18.1 copy.26
  2356.1 41.8 %all-reduce.15.cloned.1.call-done = bf16[256,3584]{1,0:T(8,128)(2,1)} async-done(((bf16[256,3584]{1,0:T(8,128)(2,1)}), bf16[256,3584]{1,0:T(8,128)(2,1)}) %all-reduce.15.cloned.1.call-update) | async-done | bytes 1835024 | tf_op jit(solution)/shard_map/psum | solution.py:12
  2397.9 26.2 %and_select_fusion.5 = bf16[1792,3584]{1,0:T(8,128)(2,1)} fusion(bf16[1792,3584]{1,0:T(8,128)(2,1)} %bitcast.98, bf16[1792,3584]{1,0:T(8,128)(2,1)} %copy.26, pred[3584]{0:T(1024)(128)(4,1)S(1)} %fusion.51, pred[3584]{0:T(1024)(128)(4,1)S(1)} %fusion.54, pred[1792]{0:T(1024)(128)(4,1)S(1)} %fusion.60, pred[1792]{0:T(1024)(128)(4,1)S(1)} %fusion.63, ...), kind=kOutput, calls=%fused_computation.73 | convolution fusion | flops 3346137088 | bytes 54143488 | tf_op jit(solution)/shard_map/dot_general | solution.py:98
  (9238 shorter events, 1790.3 us)
Async XLA Ops:
  6.5 147.2 %all-reduce.7.cloned.1.call-start = ((), (), s32[]{:S(2)}) async-start(), calls=%async_computation | async-start | bytes 262144 | tf_op jit(solution)/shard_map/psum | solution.py:12
  8.1 1118.4 %all-reduce.11.cloned.1.call-start = ((), (), s32[]{:S(2)}) async-start(), calls=%async_computation.2 | async-start | bytes 1835008 | tf_op jit(solution)/shard_map/psum | solution.py:12
  994.7 199.0 %all-reduce.9.cloned.1.call-start = ((), (), s32[]{:S(2)}) async-start(), calls=%async_computation.1 | async-start | bytes 3670016 | tf_op jit(solution)/shard_map/psum | solution.py:12
  1105.6 253.2 %all-reduce.13.cloned.1.call-start = ((), (), s32[]{:S(2)}) async-start(), calls=%async_computation.3 | async-start | bytes 262144 | tf_op jit(solution)/shard_map/psum | solution.py:12
  1133.6 60.0 %copy-start.1 = (bf16[1792,256]{0,1:T(8,128)(2,1)S(1)}, bf16[1792,256]{0,1:T(8,128)(2,1)}, u32[]{:S(2)}) copy-start(bf16[1792,256]{0,1:T(8,128)(2,1)} %all-reduce.11.cloned.1.call-done) | copy-start | bytes 2752516
  1215.0 4.6 copy-start.2
  1220.3 1110.4 %all-reduce.17.cloned.1.call-start = ((), (), s32[]{:S(2)}) async-start(), calls=%async_computation.5 | async-start | bytes 1835008 | tf_op jit(solution)/shard_map/psum | solution.py:12
  2199.1 198.9 %all-reduce.15.cloned.1.call-start = ((), (), s32[]{:S(2)}) async-start(), calls=%async_computation.4 | async-start | bytes 3670016 | tf_op jit(solution)/shard_map/psum | solution.py:12
  2338.0 59.9 %copy-start = (bf16[1792,256]{1,0:T(8,128)(2,1)S(1)}, bf16[1792,256]{1,0:T(8,128)(2,1)}, u32[]{:S(2)}) copy-start(bf16[1792,256]{1,0:T(8,128)(2,1)} %all-reduce.17.cloned.1.call-done) | copy-start | bytes 2752516
Sparse Core Ops, SparseCore 0:
  12.1 141.5 all-reduce.6
  994.8 56.5 all-reduce.10
  1105.7 87.8 all-reduce.8
  1220.4 138.3 all-reduce.12
  2199.2 56.5 all-reduce.16
  2310.1 87.8 all-reduce.14
where the time goes:
time: 2450 us; the launch traced here: 2430 us
  other arithmetic  1530 us (62%)
  waiting for transfers between devices  368 us (15%)
  matrix products  259 us (11%)
  local copies, waits for them, and re-layouts  175 us (7%)
  loops' own time  82.9 us (3%)
    psum x6, waiting for transfers between devices, broadcast(): return lax.psum(block, axis)  367 us
    div x512, other arithmetic, substitute(): (unit - jnp.dot(strict, inverse, precision=lax.Precision.HIGHEST)) / pivot  354 us
    select_n x512, other arithmetic, eliminate(): kept = jnp.where(positions > column, scaled, values)  335 us
    reduce_sum x512, other arithmetic, eliminate(): pivot = jnp.sum(jnp.where(positions == column, pivot_row, 0.0))  307 us
    reduce_sum x512, other arithmetic, substitute(): pivot = jnp.sum(jnp.where(positions == index, line, 0.0))  307 us
    select_n x1024, other arithmetic, substitute(): return jnp.where(positions[:, None] == index, fresh[None, :], inverse)  114 us
    dot_general x512, matrix products, substitute(): fresh = unit - jnp.dot(strict, inverse, precision=lax.Precision.HIGHEST)  98.2 us
    dot_general x512, matrix products, substitute(): jnp.dot(strict, inverse, precision=lax.Precision.HIGHEST)  97 us

commit v1 on v0

v1 whole, which is shorter than its diff:
```python
import functools
import jax, jax.numpy as jnp
from jax import lax
from jax.experimental import pallas as pl
from jax.experimental.pallas import tpu as pltpu
from jax.sharding import PartitionSpec as P
NB=256
F=jnp.float32
BF=jnp.bfloat16

def split2(x):
    hi=x.astype(BF); lo=(x-hi.astype(F)).astype(BF)
    return hi,lo
def dotT(a,b):
    return lax.dot_general(a,b,(((1,),(1,)),((),())),preferred_element_type=F)

def sub_bcast(x,i):
    return jnp.broadcast_to(x[i:i+1,:],(8,128))

def recip(p):
    r=pl.reciprocal(p,approx=True)
    r=r*(2.0-p*r)
    r=r*(2.0-p*r)
    return r

def panel(q, PR, PT, sub, lane):
    base=(q%4)*32
    hi=(q>=4)
    E=[jnp.where(lane==base+8*g+sub,1.0,0.0).astype(F) for g in range(4)]
    E2=list(E)
    rpv=[jnp.zeros((8,128),F) for _ in range(4)]
    for s in range(4):
        idx=[jnp.full((8,128),base+8*s+m,jnp.int32) for m in range(8)]
        R=[[None]*4 for _ in range(8)]; Q=[[None]*4 for _ in range(8)]
        for g in range(s,4):
            tr=jnp.where(hi,PR[g][1],PR[g][0]); tt=jnp.where(hi,PT[g][1],PT[g][0])
            for m in range(8):
                R[m][g]=jnp.take_along_axis(tr,idx[m],axis=1,mode="promise_in_bounds")
                Q[m][g]=jnp.take_along_axis(tt,idx[m],axis=1,mode="promise_in_bounds")
        for i in range(8):
            rp=recip(sub_bcast(R[i][s],i))
            rpv[s]=jnp.where(sub==i,rp,rpv[s])
            pr=[sub_bcast(PR[s][h],i) for h in range(2)]+[sub_bcast(E[s],i)]
            pt=[sub_bcast(PT[s][h],i) for h in range(2)]+[sub_bcast(E2[s],i)]
            rb={m:sub_bcast(R[m][s],i) for m in range(i+1,8)}
            qb={m:sub_bcast(Q[m][s],i) for m in range(i+1,8)}
            for g in range(s,4):
                l=R[i][g]*rp; u=Q[i][g]*rp
                if g==s:
                    if i==7: continue
                    l=jnp.where(sub>i,l,0.0); u=jnp.where(sub>i,u,0.0)
                for m in range(i+1,8):
                    R[m][g]=R[m][g]-l*rb[m]
                    Q[m][g]=Q[m][g]-u*qb[m]
                for h in range(2):
                    PR[g][h]=PR[g][h]-l*pr[h]
                    PT[g][h]=PT[g][h]-u*pt[h]
                E[g]=E[g]-l*pr[2]
                E2[g]=E2[g]-u*pt[2]
    return PR,PT,E,E2,rpv

def rank_update(ref, XT, Y, inp):
    xh,xl=split2(XT); yh,yl=split2(Y)
    X=jnp.concatenate([xh,xh,xl],axis=0)
    Y3=jnp.concatenate([yh,yl,yh],axis=0)
    up=lax.dot_general(X,Y3,(((0,),(0,)),((),())),preferred_element_type=F)
    ref[...]=jnp.where(inp,0.0,ref[...])-up

def lu_inv(a_bf, W, V, U, LT, LI, UT, hooks=()):
    r0=lax.broadcasted_iota(jnp.int32,(256,256),0); c0=lax.broadcasted_iota(jnp.int32,(256,256),1)
    eye=jnp.where(r0==c0,1.0,0.0).astype(BF)
    W[...]=a_bf.astype(F)
    V[...]=dotT(eye,a_bf)
    sub=lax.broadcasted_iota(jnp.int32,(8,128),0); lane=lax.broadcasted_iota(jnp.int32,(8,128),1)
    def body(q,_):
        for at, hook in hooks:
            pl.when(q==at)(hook)
        o=pl.multiple_of(q*32,32)
        PR=[[W[pl.ds(o+8*g,8),128*h:128*h+128] for h in range(2)] for g in range(4)]
        PT=[[V[pl.ds(o+8*g,8),128*h:128*h+128] for h in range(2)] for g in range(4)]
        PR,PT,E,E2,rpv=panel(q,PR,PT,sub,lane)
        XL=[];XU=[];YR=[];YT=[]
        for g in range(4):
            a=[];b=[];c=[];d=[]
            for h in range(2):
                gl=lane+128*h
                inp=(gl>=o)&(gl<o+32); right=gl>=o+32; left=gl<o
                ur=PR[g][h]; ut=PT[g][h]
                lt=ut*rpv[g]; un=ur*rpv[g]
                U[pl.ds(o+8*g,8),128*h:128*h+128]=ur
                LT[pl.ds(o+8*g,8),128*h:128*h+128]=lt
                mr=jnp.where(inp,E[g],ur); mt=jnp.where(inp,E2[g],ut)
                LI[pl.ds(o+8*g,8),128*h:128*h+128]=jnp.where(right,0.0,mr)
                UT[pl.ds(o+8*g,8),128*h:128*h+128]=jnp.where(right,0.0,mt*rpv[g])
                a.append(jnp.where(right,lt,0.0)); b.append(jnp.where(right,un,0.0)); c.append(mr); d.append(mt)
            XL.append(jnp.concatenate(a,1)); XU.append(jnp.concatenate(b,1)); YR.append(jnp.concatenate(c,1)); YT.append(jnp.concatenate(d,1))
        XL=jnp.concatenate(XL,0);XU=jnp.concatenate(XU,0);YR=jnp.concatenate(YR,0);YT=jnp.concatenate(YT,0)
        inp=(c0>=o)&(c0<o+32)
        rank_update(W,XL,YR,inp)
        rank_update(V,XU,YT,inp)
        return 0
    lax.fori_loop(0,8,body,0)

def finish(U,LT,pk):
    r0=lax.broadcasted_iota(jnp.int32,(256,256),0); c0=lax.broadcasted_iota(jnp.int32,(256,256),1)
    eye=jnp.where(r0==c0,1.0,0.0).astype(BF)
    low=dotT(eye,LT[...].astype(BF))
    pk[...]=jnp.where(r0>c0,low,U[...]).astype(BF)


NR=16
NC=8
PC=16
MESH=pl.DeviceIdType.MESH

def front_kernel(mat, Lraw, Traw, pk0, pk1, li0, ut0, li1, ut1, l10, t01,
                 corner, W, V, U, LT, LI, UT,
                 c1s, c1r, c2s, c2r, c3s, c3r, d3s, d3r, tss, tsr, tgs, tgr, lss, lsr, lgs, lgr, loc):
    row=lax.axis_index("row"); col=lax.axis_index("col")
    cols=mat.shape[1]
    PL=mat.shape[0]//NC

    def rp_(j): return lax.rem(row+j,NR)
    def cp_(j): return lax.rem(col+j,NC)
    def rows(k,n=PC): return pl.ds(pl.multiple_of(k*n,n),n)
    def rc(src,dst,ss,rs,**dev):
        return pltpu.make_async_remote_copy(src_ref=src,dst_ref=dst,send_sem=ss,recv_sem=rs,device_id=dev,device_id_type=MESH)
    def loop(n,f):
        def b(j,_):
            f(j); return 0
        lax.fori_loop(1,n,b,0)

    bar=pltpu.get_barrier_semaphore()
    loop(NR,lambda j: pl.semaphore_signal(bar,inc=1,device_id={"row":rp_(j)},device_id_type=MESH))
    loop(NC,lambda j: pl.semaphore_signal(bar,inc=1,device_id={"col":cp_(j)},device_id_type=MESH))
    pl.semaphore_wait(bar,NR-1+NC-1)

    def own_corner(i,b,k): return mat.at[rows(k),0:NB], corner.at[b,rows(k)]
    def c1(i,jj,j):
        k=rp_(j); s,d=own_corner(i,2*i+jj,k)
        return rc(s,d,c1s.at[j],c1r.at[i],row=k)
    for i in range(2):
        for jj in range(2):
            @pl.when((row==i)&(col==jj))
            def _(i=i,jj=jj):
                s,d=own_corner(i,2*i+jj,row)
                pltpu.make_async_copy(s,d,loc.at[0]).start()
                loop(NR,lambda j: c1(i,jj,j).start())
                pltpu.make_async_copy(s,d,loc.at[0]).wait()
    def c2(i,jj,j):
        b=2*i+jj
        return rc(corner.at[b,rows(row)],corner.at[b,rows(row)],c2s.at[i,j],c2r.at[b],col=cp_(j))
    def c3(j):
        k=rp_(j); return rc(corner.at[0,rows(row)],corner.at[0,rows(row)],c3s.at[j],c3r.at[row],row=k)
    def d3(j):
        k=rp_(j); return rc(corner.at[1:4,rows(row)],corner.at[1:4,rows(row)],d3s.at[j],d3r.at[row],row=k)
    def c3w(j):
        k=rp_(j); rc(corner.at[0,rows(k)],corner.at[0,rows(k)],c3s.at[j],c3r.at[k],row=k).wait_recv()
    def d3w(j):
        k=rp_(j); rc(corner.at[1:4,rows(k)],corner.at[1:4,rows(k)],d3s.at[j],d3r.at[k],row=k).wait_recv()
    for i in range(2):
        for jj in range(2):
            @pl.when(col==jj)
            def _(i=i,jj=jj):
                @pl.when(row!=i)
                def _():
                    c1(i,jj,1).wait_recv()
                loop(NC,lambda j: c2(i,jj,j).start())
        if i==0:
            @pl.when(col!=0)
            def _(): c2(0,0,1).wait_recv()
            loop(NR,lambda j: c3(j).start())
    def ts(i,j):
        k=rp_(j); return rc(mat.at[rows(k)],Traw.at[i,rows(k)],tss.at[j],tsr.at[i],row=k)
    def ls(i,j):
        k=cp_(j); return rc(mat.at[rows(k,PL),0:NB],Lraw.at[i,rows(k,PL)],lss.at[j],lsr.at[i],col=k)
    def tl(i): return pltpu.make_async_copy(mat.at[rows(row)],Traw.at[i,rows(row)],loc.at[1])
    def ll(i): return pltpu.make_async_copy(mat.at[rows(col,PL),0:NB],Lraw.at[i,rows(col,PL)],loc.at[2])
    for i in range(2):
        @pl.when(row==i)
        def _(i=i):
            tl(i).start(); loop(NR,lambda j: ts(i,j).start())
        @pl.when(col==i)
        def _(i=i):
            ll(i).start(); loop(NC,lambda j: ls(i,j).start())
    for b in (1,2,3):
        @pl.when(col!=b%2)
        def _(b=b): c2(b//2,b%2,1).wait_recv()
    loop(NR,lambda j: d3(j).start())
    loop(NR,c3w)

    def tg(i,j):
        k=rp_(j); return rc(Traw.at[i,rows(row)],Traw.at[i,rows(row)],tgs.at[i,j],tgr.at[i,row],row=k)
    def lg(i,j):
        k=cp_(j); return rc(Lraw.at[i,rows(col,PL)],Lraw.at[i,rows(col,PL)],lgs.at[i,j],lgr.at[i,col],col=k)
    def tgw(i,j):
        k=rp_(j); rc(Traw.at[i,rows(k)],Traw.at[i,rows(k)],tgs.at[i,j],tgr.at[i,k],row=k).wait_recv()
    def lgw(i,j):
        k=cp_(j); rc(Lraw.at[i,rows(k,PL)],Lraw.at[i,rows(k,PL)],lgs.at[i,j],lgr.at[i,k],col=k).wait_recv()
    def gather(i):
        @pl.when(col==i)
        def _(): ll(i).wait()
        @pl.when(col!=i)
        def _(): ls(i,1).wait_recv()
        loop(NC,lambda j: lg(i,j).start())
        @pl.when(row==i)
        def _(): tl(i).wait()
        @pl.when(row!=i)
        def _(): ts(i,1).wait_recv()
        loop(NR,lambda j: tg(i,j).start())

    def dump(li,ut):
        for ref,src in ((li,LI),(ut,UT)):
            for n,x in enumerate(split2(src[...])): ref[n]=x
    lu_inv(corner[0],W,V,U,LT,LI,UT,((HOOK0,lambda: gather(0)),(HOOK1,lambda: gather(1))))
    finish(U,LT,pk0); dump(li0,ut0)
    loop(NR,d3w)
    L=sum(dotT(corner[2],ut0[n]) for n in (1,0)).astype(BF)
    T=sum(jnp.dot(li0[n],corner[1],preferred_element_type=F) for n in (1,0)).astype(BF)
    l10[...]=L; t01[...]=T
    a=(corner[3].astype(F)-jnp.dot(L,T,preferred_element_type=F)).astype(BF)
    lu_inv(a,W,V,U,LT,LI,UT)
    finish(U,LT,pk1); dump(li1,ut1)
    for i in range(2):
        loop(NC,lambda j: lgw(i,j))
        loop(NR,lambda j: tgw(i,j))
    for i in range(2):
        for jj in range(2):
            @pl.when((row==i)&(col==jj))
            def _(i=i,jj=jj): loop(NR,lambda j: c1(i,jj,j).wait_send())
            @pl.when(col==jj)
            def _(i=i,jj=jj): loop(NC,lambda j: c2(i,jj,j).wait_send())
        @pl.when(row==i)
        def _(i=i): loop(NR,lambda j: ts(i,j).wait_send())
        @pl.when(col==i)
        def _(i=i): loop(NC,lambda j: ls(i,j).wait_send())
        loop(NC,lambda j: lg(i,j).wait_send())
        loop(NR,lambda j: tg(i,j).wait_send())
    loop(NR,lambda j: c3(j).wait_send())
    loop(NR,lambda j: d3(j).wait_send())

HOOK0=3
HOOK1=5

def front(mat):
    rows_,cols_=mat.shape
    vm=pl.BlockSpec(memory_space=pltpu.VMEM); an=pl.BlockSpec(memory_space=pl.ANY)
    s=jax.ShapeDtypeStruct((NB,NB),BF); s2=jax.ShapeDtypeStruct((2,NB,NB),BF)
    dma=pltpu.SemaphoreType.DMA
    return pl.pallas_call(front_kernel,
        out_shape=[jax.ShapeDtypeStruct((2,rows_,NB),BF),jax.ShapeDtypeStruct((2,NB,cols_),BF),s,s,s2,s2,s2,s2,s,s],
        in_specs=[an],out_specs=[an,an]+[vm]*8,
        scratch_shapes=[pltpu.VMEM((4,NB,NB),BF)]+[pltpu.VMEM((NB,NB),F)]*6+[
            dma((NR,)),dma((2,)),dma((2,NC)),dma((4,)),dma((NR,)),dma((NR,)),dma((NR,)),dma((NR,)),
            dma((NR,)),dma((2,)),dma((2,NR)),dma((2,NR)),dma((NC,)),dma((2,)),dma((2,NC)),dma((2,NC)),dma((3,))],
        compiler_params=pltpu.CompilerParams(collective_id=0,has_side_effects=True,vmem_limit_bytes=40*2**20))(mat)

def update_kernel(a, lraw, traw, pk0, pk1, li0, ut0, li1, ut1, l10, t01, out, T0, T1):
    t=pl.program_id(0)
    row=lax.axis_index("row"); col=lax.axis_index("col")
    cols=a.shape[1]
    CH=cols//7
    def mm(x,y): return jnp.dot(x,y,preferred_element_type=F)
    @pl.when(t==0)
    def _():
        for c in range(7):
            w=pl.ds(c*CH,CH)
            x=traw[0,:,w]
            y=(mm(li0[1],x)+mm(li0[0],x)).astype(BF)
            T0[:,w]=y
            z=(traw[1,:,w].astype(F)-mm(l10[...],y)).astype(BF)
            T1[:,w]=(mm(li1[1],z)+mm(li1[0],z)).astype(BF)
    x=lraw[0]
    L0=(dotT(x,ut0[1])+dotT(x,ut0[0])).astype(BF)
    z=(lraw[1].astype(F)-mm(L0,t01[...])).astype(BF)
    L1=(dotT(z,ut1[1])+dotT(z,ut1[0])).astype(BF)
    for c in range(7):
        w=pl.ds(c*CH,CH)
        y=(a[:,w].astype(F)-mm(L0,T0[:,w])).astype(BF)
        out[:,w]=(y.astype(F)-mm(L1,T1[:,w])).astype(BF)
    @pl.when(col==0)
    def _(): out[:,0:NB]=L0
    @pl.when(col==1)
    def _(): out[:,0:NB]=L1
    @pl.when((t==0)&(row==0))
    def _():
        out[...]=T0[...]
        @pl.when(col==0)
        def _(): out[:,0:NB]=pk0[...]
    @pl.when((t==0)&(row==1))
    def _():
        out[:,NB:]=T1[:,NB:]
        @pl.when(col==1)
        def _(): out[:,0:NB]=pk1[...]
        @pl.when(col>1)
        def _(): out[:,0:NB]=T1[:,0:NB]

def update(mat, Lraw, Traw, *small):
    rows_,cols_=mat.shape
    vm=pl.BlockSpec(memory_space=pltpu.VMEM)
    return pl.pallas_call(update_kernel,grid=(rows_//NB,),
        out_shape=jax.ShapeDtypeStruct(mat.shape,BF),
        in_specs=[pl.BlockSpec((NB,cols_),lambda t:(t,0)),pl.BlockSpec((2,NB,NB),lambda t:(0,t,0)),vm]+[vm]*8,
        out_specs=pl.BlockSpec((NB,cols_),lambda t:(t,0)),
        scratch_shapes=[pltpu.VMEM((NB,cols_),BF)]*2,
        compiler_params=pltpu.CompilerParams(vmem_limit_bytes=50*2**20))(mat,Lraw,Traw,*small)

def on_device(mat):
    return update(mat,*front(mat))

def solution(mesh):
    return jax.shard_map(on_device,mesh=mesh,in_specs=(P("row","col"),),out_specs=P("row","col"),check_vma=False)
```

time: 2450 us -> 109 us (0.04)
  the two profiles are of different devices: /device:TPU:4 before, /device:TPU:2 now
where the time goes in v1:
time: 109 us; the launch traced here: 108 us
  Pallas kernels  106 us (97%)
  local copies, waits for them, and re-layouts  1.78 us (2%)
    pallas_call x1, Pallas kernels, front(): pl.pallas_call(front_kernel, out_shape=[jax.ShapeDtypeStruct((2, rows_, N...  84.9 us
    pallas_call x1, Pallas kernels, update(): pl.pallas_call(update_kernel, grid=(rows_ // NB,), out_shape=jax.ShapeDty...  21.5 us

profile of v1, /device:TPU:2, one launch (start us, length us, event | category | flops | bytes accessed | tf_op | source)
XLA Modules:
  0.0 108.2 jit_solution(10297459117133507572)
XLA Ops:
  0.0 84.9 %shard_map.17 = (bf16[2,1792,256]{2,1,0:T(8,128)(2,1)S(1)}, bf16[2,256,3584]{2,1,0:T(8,128)(2,1)S(1)}, bf16[256,256]{1,0:T(8,128)(2,1)S(1)}, bf16[256,256]{1,0:T...) custom-call(bf16[1792,3584]{1,0:T(8,128)(2,1)} %a.1), custom_call_target="tpu_custom_call" | custom-call | tf_op jit(solution)/shard_map/pallas_call | solution.py:250
  84.9 0.0 copy-start
  84.9 1.8 %copy-done = bf16[2,256,3584]{2,1,0:T(8,128)(2,1)} copy-done((bf16[2,256,3584]{2,1,0:T(8,128)(2,1)}, bf16[2,256,3584]{2,1,0:T(8,128)(2,1)S(1)}, u32[]{:S(2)}) %copy-start) | copy-done | bytes 3670040
  86.7 21.5 %shard_map.18 = bf16[1792,3584]{1,0:T(8,128)(2,1)} custom-call(bf16[1792,3584]{1,0:T(8,128)(2,1)} %a.1, bf16[2,1792,256]{2,1,0:T(8,128)(2,1)S(1)} %get-tuple-element.15.lraw, bf16[2,256,3584]{2,1,0:T(8,128)(2,1)} %copy-done, bf16[256,256]{1,0:T(8,128)(2,1)S(1)} %get-tuple-element.17.pk0, bf16[256,256]{1,0:T(8,128)(2,1)S(1)} %get-tuple-element.18.pk1, ...), custom_call_target="tpu_custom_call" | custom-call | tf_op jit(solution)/shard_map/pallas_call | solution.py:301
Async XLA Ops:
  84.9 1.8 %copy-start = (bf16[2,256,3584]{2,1,0:T(8,128)(2,1)}, bf16[2,256,3584]{2,1,0:T(8,128)(2,1)S(1)}, u32[]{:S(2)}) copy-start(bf16[2,256,3584]{2,1,0:T(8,128)(2,1)S(1)} %get-tuple-element.16.traw) | copy-start | bytes 11010052

commit v2 on v1

v2 whole, which is shorter than its diff:
```python
import functools
import jax, jax.numpy as jnp
from jax import lax
from jax.experimental import pallas as pl
from jax.experimental.pallas import tpu as pltpu
from jax.sharding import PartitionSpec as P
NB=256
F=jnp.float32
BF=jnp.bfloat16

def split2(x):
    hi=x.astype(BF); lo=(x-hi.astype(F)).astype(BF)
    return hi,lo
def dotT(a,b):
    return lax.dot_general(a,b,(((1,),(1,)),((),())),preferred_element_type=F)

def sub_bcast(x,i):
    return jnp.broadcast_to(x[i:i+1,:],(8,128))

def recip(p):
    r=pl.reciprocal(p,approx=True)
    r=r*(2.0-p*r)
    r=r*(2.0-p*r)
    return r

def panel(q, PR, PT, sub, lane):
    base=(q%4)*32
    hi=(q>=4)
    E=[jnp.where(lane==base+8*g+sub,1.0,0.0).astype(F) for g in range(4)]
    E2=list(E)
    rpv=[jnp.zeros((8,128),F) for _ in range(4)]
    for s in range(4):
        idx=[jnp.full((8,128),base+8*s+m,jnp.int32) for m in range(8)]
        R=[[None]*4 for _ in range(8)]; Q=[[None]*4 for _ in range(8)]
        for g in range(s,4):
            tr=jnp.where(hi,PR[g][1],PR[g][0]); tt=jnp.where(hi,PT[g][1],PT[g][0])
            for m in range(8):
                R[m][g]=jnp.take_along_axis(tr,idx[m],axis=1,mode="promise_in_bounds")
                Q[m][g]=jnp.take_along_axis(tt,idx[m],axis=1,mode="promise_in_bounds")
        for i in range(8):
            rp=recip(sub_bcast(R[i][s],i))
            rpv[s]=jnp.where(sub==i,rp,rpv[s])
            pr=[sub_bcast(PR[s][h],i) for h in range(2)]+[sub_bcast(E[s],i)]
            pt=[sub_bcast(PT[s][h],i) for h in range(2)]+[sub_bcast(E2[s],i)]
            rb={m:sub_bcast(R[m][s],i) for m in range(i+1,8)}
            qb={m:sub_bcast(Q[m][s],i) for m in range(i+1,8)}
            for g in range(s,4):
                l=R[i][g]*rp; u=Q[i][g]*rp
                if g==s:
                    if i==7: continue
                    l=jnp.where(sub>i,l,0.0); u=jnp.where(sub>i,u,0.0)
                for m in range(i+1,8):
                    R[m][g]=R[m][g]-l*rb[m]
                    Q[m][g]=Q[m][g]-u*qb[m]
                for h in range(2):
                    PR[g][h]=PR[g][h]-l*pr[h]
                    PT[g][h]=PT[g][h]-u*pt[h]
                E[g]=E[g]-l*pr[2]
                E2[g]=E2[g]-u*pt[2]
    return PR,PT,E,E2,rpv

def rank_update(ref, XT, Y, inp):
    xh,xl=split2(XT); yh,yl=split2(Y)
    X=jnp.concatenate([xh,xh,xl],axis=0)
    Y3=jnp.concatenate([yh,yl,yh],axis=0)
    up=lax.dot_general(X,Y3,(((0,),(0,)),((),())),preferred_element_type=F)
    ref[...]=jnp.where(inp,0.0,ref[...])-up

def lu_inv(a_bf, W, V, U, LT, LI, UT, hooks=()):
    r0=lax.broadcasted_iota(jnp.int32,(256,256),0); c0=lax.broadcasted_iota(jnp.int32,(256,256),1)
    eye=jnp.where(r0==c0,1.0,0.0).astype(BF)
    W[...]=a_bf.astype(F)
    V[...]=dotT(eye,a_bf)
    sub=lax.broadcasted_iota(jnp.int32,(8,128),0); lane=lax.broadcasted_iota(jnp.int32,(8,128),1)
    def body(q,_):
        for at, hook in hooks:
            pl.when(q==at)(hook)
        o=pl.multiple_of(q*32,32)
        PR=[[W[pl.ds(o+8*g,8),128*h:128*h+128] for h in range(2)] for g in range(4)]
        PT=[[V[pl.ds(o+8*g,8),128*h:128*h+128] for h in range(2)] for g in range(4)]
        PR,PT,E,E2,rpv=panel(q,PR,PT,sub,lane)
        XL=[];XU=[];YR=[];YT=[]
        for g in range(4):
            a=[];b=[];c=[];d=[]
            for h in range(2):
                gl=lane+128*h
                inp=(gl>=o)&(gl<o+32); right=gl>=o+32; left=gl<o
                ur=PR[g][h]; ut=PT[g][h]
                lt=ut*rpv[g]; un=ur*rpv[g]
                U[pl.ds(o+8*g,8),128*h:128*h+128]=ur
                LT[pl.ds(o+8*g,8),128*h:128*h+128]=lt
                mr=jnp.where(inp,E[g],ur); mt=jnp.where(inp,E2[g],ut)
                LI[pl.ds(o+8*g,8),128*h:128*h+128]=jnp.where(right,0.0,mr)
                UT[pl.ds(o+8*g,8),128*h:128*h+128]=jnp.where(right,0.0,mt*rpv[g])
                a.append(jnp.where(right,lt,0.0)); b.append(jnp.where(right,un,0.0)); c.append(mr); d.append(mt)
            XL.append(jnp.concatenate(a,1)); XU.append(jnp.concatenate(b,1)); YR.append(jnp.concatenate(c,1)); YT.append(jnp.concatenate(d,1))
        XL=jnp.concatenate(XL,0);XU=jnp.concatenate(XU,0);YR=jnp.concatenate(YR,0);YT=jnp.concatenate(YT,0)
        inp=(c0>=o)&(c0<o+32)
        rank_update(W,XL,YR,inp)
        rank_update(V,XU,YT,inp)
        return 0
    lax.fori_loop(0,8,body,0)

def finish(U,LT,pk):
    r0=lax.broadcasted_iota(jnp.int32,(256,256),0); c0=lax.broadcasted_iota(jnp.int32,(256,256),1)
    eye=jnp.where(r0==c0,1.0,0.0).astype(BF)
    low=dotT(eye,LT[...].astype(BF))
    pk[...]=jnp.where(r0>c0,low,U[...]).astype(BF)


NR=16
NC=8
NY=4
CP=NB//NC
MESH=pl.DeviceIdType.MESH
AT=dict(d3=(1,),lg=(2,),s2=(3,1),g1=(6,4),g2=(8,6))

def front_kernel(mat, Lout, Tout, pk0, pk1,
                 Lraw, Traw, li0, ut0, li1, ut1, l10, t01, corner, W, V, U, LT, LI, UT,
                 p1s, p1r, p2s, p2r, c3s, c3r, d3s, d3r, lss, lsr, lgs, lgr,
                 s1s, s1r, s2s, s2p, s2r, g1s, g1r, g2s, g2r, loc):
    row=lax.axis_index("row"); col=lax.axis_index("col")
    y=lax.rem(row,NY); z=row//NY
    cols=mat.shape[1]
    PL=mat.shape[0]//NC
    H=cols//2

    def rp_(j): return lax.rem(row+j,NR)
    def cp_(j): return lax.rem(col+j,NC)
    def rows(k,n): return pl.ds(pl.multiple_of(k*n,n),n)
    def rc(src,dst,ss,rs,**dev):
        return pltpu.make_async_remote_copy(src_ref=src,dst_ref=dst,send_sem=ss,recv_sem=rs,device_id=dev,device_id_type=MESH)
    def loop(n,f):
        def b(j,_):
            f(j); return 0
        lax.fori_loop(1,n,b,0)

    bar=pltpu.get_barrier_semaphore()
    loop(NR,lambda j: pl.semaphore_signal(bar,inc=1,device_id={"row":rp_(j)},device_id_type=MESH))
    loop(NC,lambda j: pl.semaphore_signal(bar,inc=1,device_id={"col":cp_(j)},device_id_type=MESH))
    pl.semaphore_wait(bar,NR-1+NC-1)

    Q=NB//NY; PC=Q//NY
    def nx(v,d): return lax.rem(v+d,NY)
    def half(h): return slice(0,H) if h==0 else slice(H,2*H)
    def ab(h): return (z,y) if h==0 else (y,z)
    def dev(h,a,b): return a*NY+b if h==0 else b*NY+a
    def qref(ref,h,a): return ref.at[rows(a,Q),half(h)]
    def tq(i,h,a): return Traw.at[i,rows(a,Q),half(h)]
    def s1(i,h,d):
        a,b=ab(h); a2=nx(a,d)
        return rc(qref(mat,h,a2),tq(i,h,a2),s1s.at[h,d],s1r.at[i,h],row=dev(h,a2,b))
    def s1l(i,h):
        a,b=ab(h); return pltpu.make_async_copy(qref(mat,h,a),tq(i,h,a),loc.at[1+h])
    def scatter(i):
        @pl.when(row==i)
        def _():
            for h in range(2):
                s1l(i,h).start(); loop(NY,lambda d: s1(i,h,d).start())
    def p1(b,j):
        c=cp_(j); return rc(mat.at[rows(c,CP),0:NB],corner.at[b,rows(c,CP)],p1s.at[j],p1r.at[b%2],col=c)
    def p1w(b):
        pl.when(col!=b%2)(lambda: p1(b,1).wait_recv())
    for i in range(2):
        for jj in range(2):
            @pl.when((row==i)&(col==jj))
            def _(b=2*i+jj):
                cc=pltpu.make_async_copy(mat.at[rows(col,CP),0:NB],corner.at[b,rows(col,CP)],loc.at[0])
                cc.start()
                loop(NC,lambda j: p1(b,j).start())
                cc.wait()
    scatter(1)
    mine=rows(col,CP)
    def p2(n,j):
        r=(corner.at[0,mine],corner.at[1,mine],corner.at[2:4,mine])[n]
        return rc(r,r,p2s.at[n,j],p2r.at[n],row=rp_(j))
    def c3(j): return rc(corner.at[0,mine],corner.at[0,mine],c3s.at[j],c3r.at[col],col=cp_(j))
    def d3(j): return rc(corner.at[1:4,mine],corner.at[1:4,mine],d3s.at[j],d3r.at[col],col=cp_(j))
    def c3w(j):
        c=cp_(j); rc(corner.at[0,rows(c,CP)],corner.at[0,rows(c,CP)],c3s.at[j],c3r.at[c],col=c).wait_recv()
    def d3w(j):
        c=cp_(j); rc(corner.at[1:4,rows(c,CP)],corner.at[1:4,rows(c,CP)],d3s.at[j],d3r.at[c],col=c).wait_recv()
    @pl.when(row==0)
    def _():
        p1w(0); loop(NR,lambda j: p2(0,j).start())
    @pl.when(row!=0)
    def _(): p2(0,1).wait_recv()
    loop(NC,lambda j: c3(j).start())

    def ls(i,j):
        k=cp_(j); return rc(mat.at[rows(k,PL),0:NB],Lraw.at[i,rows(k,PL)],lss.at[j],lsr.at[i],col=k)
    def ll(i): return pltpu.make_async_copy(mat.at[rows(col,PL),0:NB],Lraw.at[i,rows(col,PL)],loc.at[3])
    def lg(i,j):
        k=cp_(j); return rc(Lraw.at[i,rows(col,PL)],Lraw.at[i,rows(col,PL)],lgs.at[i,j],lgr.at[i,col],col=k)
    def lgw(i,j):
        k=cp_(j); rc(Lraw.at[i,rows(k,PL)],Lraw.at[i,rows(k,PL)],lgs.at[i,j],lgr.at[i,k],col=k).wait_recv()
    def left_gather():
        for i in range(2):
            pl.when(col==i)(lambda: ll(i).wait())
            pl.when(col!=i)(lambda: ls(i,1).wait_recv())
            loop(NC,lambda j: lg(i,j).start())

    def src_ab(h,i): return (0,i) if h==0 else (i,0)
    def tp(i,h,a,b): return Traw.at[i,rows(a*NY+b,PC),half(h)]
    def s2(i,h,d):
        a,b=ab(h); b2=nx(b,d)
        return rc(tp(i,h,a,b2),tp(i,h,a,b2),s2s.at[i,h,d],s2r.at[i,h],row=dev(h,a,b2))
    def g1(i,h,d,ss):
        a,b=ab(h); b2=nx(b,d)
        return rc(tp(i,h,a,b),tp(i,h,a,b),ss.at[i,h,d],g1r.at[i,h,b],row=dev(h,a,b2))
    def g1w(i,h,d):
        a,b=ab(h); b2=nx(b,d)
        rc(tp(i,h,a,b2),tp(i,h,a,b2),g1s.at[i,h,d],g1r.at[i,h,b2],row=dev(h,a,b2)).wait_recv()
    def g2(i,h,d):
        a,b=ab(h); a2=nx(a,d)
        return rc(tq(i,h,a),tq(i,h,a),g2s.at[i,h,d],g2r.at[i,h,a],row=dev(h,a2,b))
    def g2w(i,h,d):
        a,b=ab(h); a2=nx(a,d)
        rc(tq(i,h,a2),tq(i,h,a2),g2s.at[i,h,d],g2r.at[i,h,a2],row=dev(h,a2,b)).wait_recv()
    each=[(i,h) for i in range(2) for h in range(2)]
    def inner_is_src(i,h): return ab(h)[1]==src_ab(h,i)[1]
    def top_s2(n):
        for i,h in each:
            if i!=n: continue
            @pl.when(inner_is_src(i,h))
            def _(i=i,h=h):
                pl.when(row==i)(lambda: s1l(i,h).wait())
                pl.when(row!=i)(lambda: s1(i,h,1).wait_recv())
                def f(d):
                    s2(i,h,d).start(); g1(i,h,d,s2p).start()
                loop(NY,f)
    def top_g1(n):
        for i,h in each:
            if i!=n: continue
            sb=src_ab(h,i)[1]; b=ab(h)[1]
            @pl.when(b!=sb)
            def _(i=i,h=h,sb=sb,b=b):
                s2(i,h,1).wait_recv()
                loop(NY,lambda d: pl.when(nx(b,d)!=sb)(lambda: g1(i,h,d,g1s).start()))
    def top_g2(n):
        for i,h in each:
            if i!=n: continue
            @pl.when(ab(h)[1]!=src_ab(h,i)[1])
            def _(i=i,h=h): loop(NY,lambda d: g1w(i,h,d))
            loop(NY,lambda d: g2(i,h,d).start())

    for i in range(2):
        if i==0: scatter(0)
        @pl.when(col==i)
        def _(i=i):
            ll(i).start(); loop(NC,lambda j: ls(i,j).start())
    @pl.when(row==0)
    def _():
        p1w(1); loop(NR,lambda j: p2(1,j).start())
    @pl.when(row==1)
    def _():
        p1w(2); p1w(3); loop(NR,lambda j: p2(2,j).start())
    loop(NC,c3w)
    def rest_corners():
        pl.when(row!=0)(lambda: p2(1,1).wait_recv())
        pl.when(row!=1)(lambda: p2(2,1).wait_recv())
        loop(NC,lambda j: d3(j).start())

    def dump(li,ut):
        for ref,src in ((li,LI),(ut,UT)):
            for n,x in enumerate(split2(src[...])): ref[n]=x
    acts=[(AT["d3"][0],rest_corners),(AT["lg"][0],left_gather)]
    for f,n in ((top_s2,"s2"),(top_g1,"g1"),(top_g2,"g2")):
        acts+=[(AT[n][k],functools.partial(f,k)) for k in (0,1)]
    lu_inv(corner[0],W,V,U,LT,LI,UT,[x for x in acts if x[0]<8])
    finish(U,LT,pk0); dump(li0,ut0)
    loop(NC,d3w)
    L=sum(dotT(corner[2],ut0[n]) for n in (1,0)).astype(BF)
    T=sum(jnp.dot(li0[n],corner[1],preferred_element_type=F) for n in (1,0)).astype(BF)
    l10[...]=L; t01[...]=T
    a=(corner[3].astype(F)-jnp.dot(L,T,preferred_element_type=F)).astype(BF)
    lu_inv(a,W,V,U,LT,LI,UT,[(x[0]-8,x[1]) for x in acts if x[0]>=8])
    finish(U,LT,pk1); dump(li1,ut1)
    for i in range(2):
        loop(NC,lambda j: lgw(i,j))
    def mm(x,y): return jnp.dot(x,y,preferred_element_type=F)
    LB=NB
    def lsolve(k,_):
        w=pl.ds(pl.multiple_of(k*LB,LB),LB)
        x=Lraw[0,w]
        x=(dotT(x,ut0[1])+dotT(x,ut0[0])).astype(BF)
        Lout[0,w]=x
        x=(Lraw[1,w].astype(F)-mm(x,t01[...])).astype(BF)
        Lout[1,w]=(dotT(x,ut1[1])+dotT(x,ut1[0])).astype(BF)
        return 0
    lax.fori_loop(0,mat.shape[0]//LB,lsolve,0)
    TB=cols//7
    for i,h in each:
        if i==0: loop(NY,lambda d: g2w(i,h,d))
    def tsolve0(k,_):
        w=pl.ds(pl.multiple_of(k*TB,TB),TB)
        x=Traw[0,:,w]
        Tout[0,:,w]=(mm(li0[1],x)+mm(li0[0],x)).astype(BF)
        return 0
    lax.fori_loop(0,7,tsolve0,0)
    for i,h in each:
        if i==1: loop(NY,lambda d: g2w(i,h,d))
    def tsolve1(k,_):
        w=pl.ds(pl.multiple_of(k*TB,TB),TB)
        x=(Traw[1,:,w].astype(F)-mm(l10[...],Tout[0,:,w])).astype(BF)
        Tout[1,:,w]=(mm(li1[1],x)+mm(li1[0],x)).astype(BF)
        return 0
    lax.fori_loop(0,7,tsolve1,0)
    for i in range(2):
        for jj in range(2):
            pl.when((row==i)&(col==jj))(lambda: loop(NC,lambda j: p1(2*i+jj,j).wait_send()))
        pl.when(col==i)(lambda: loop(NC,lambda j: ls(i,j).wait_send()))
        loop(NC,lambda j: lg(i,j).wait_send())
    pl.when(row==0)(lambda: loop(NR,lambda j: (p2(0,j).wait_send(),p2(1,j).wait_send())))
    pl.when(row==1)(lambda: loop(NR,lambda j: p2(2,j).wait_send()))
    loop(NC,lambda j: (c3(j).wait_send(),d3(j).wait_send()))
    for i,h in each:
        b=ab(h)[1]; sb=src_ab(h,i)[1]
        pl.when(row==i)(lambda: loop(NY,lambda d: s1(i,h,d).wait_send()))
        pl.when(b==sb)(lambda: loop(NY,lambda d: (s2(i,h,d).wait_send(),g1(i,h,d,s2p).wait_send())))
        pl.when(b!=sb)(lambda: loop(NY,lambda d: pl.when(nx(b,d)!=sb)(lambda: g1(i,h,d,g1s).wait_send())))
        loop(NY,lambda d: g2(i,h,d).wait_send())

def front(mat):
    rows_,cols_=mat.shape
    vm=pl.BlockSpec(memory_space=pltpu.VMEM); an=pl.BlockSpec(memory_space=pl.ANY)
    s=jax.ShapeDtypeStruct((NB,NB),BF)
    dma=pltpu.SemaphoreType.DMA
    return pl.pallas_call(front_kernel,
        out_shape=[jax.ShapeDtypeStruct((2,rows_,NB),BF),jax.ShapeDtypeStruct((2,NB,cols_),BF),s,s],
        in_specs=[an],out_specs=[vm]*4,
        scratch_shapes=[pltpu.VMEM((2,rows_,NB),BF),pltpu.VMEM((2,NB,cols_),BF)]+[pltpu.VMEM((2,NB,NB),BF)]*4+[pltpu.VMEM((NB,NB),BF)]*2+[pltpu.VMEM((4,NB,NB),BF)]+[pltpu.VMEM((NB,NB),F)]*6+[
            dma((NC,)),dma((2,)),dma((3,NR)),dma((3,)),dma((NC,)),dma((NC,)),dma((NC,)),dma((NC,)),
            dma((NC,)),dma((2,)),dma((2,NC)),dma((2,NC)),
            dma((2,NY)),dma((2,2)),dma((2,2,NY)),dma((2,2,NY)),dma((2,2)),dma((2,2,NY)),dma((2,2,NY)),dma((2,2,NY)),dma((2,2,NY)),dma((4,))],
        compiler_params=pltpu.CompilerParams(collective_id=0,has_side_effects=True,vmem_limit_bytes=40*2**20))(mat)

def update_kernel(a, L, T, pk0, pk1, out):
    t=pl.program_id(0)
    row=lax.axis_index("row"); col=lax.axis_index("col")
    def mm(x,y): return jnp.dot(x,y,preferred_element_type=F)
    for r in range(a.shape[0]//NB):
        w=pl.ds(r*NB,NB)
        y=(a[w].astype(F)-mm(L[0,w],T[0])).astype(BF)
        out[w]=(y.astype(F)-mm(L[1,w],T[1])).astype(BF)
    for c in range(2):
        @pl.when((t==0)&(col==c))
        def _(c=c): out[:,0:NB]=L[c]
    @pl.when(row==0)
    def _():
        out[0:NB]=T[0]
        @pl.when((t==0)&(col==0))
        def _(): out[0:NB,0:NB]=pk0[...]
    @pl.when(row==1)
    def _():
        out[0:NB,NB:]=T[1,:,NB:]
        @pl.when((t>0)|(col>1))
        def _(): out[0:NB,0:NB]=T[1,:,0:NB]
        @pl.when((t==0)&(col==1))
        def _(): out[0:NB,0:NB]=pk1[...]

CW=512

def update(mat, L, T, pk0, pk1):
    rows_,cols_=mat.shape
    vm=pl.BlockSpec(memory_space=pltpu.VMEM)
    return pl.pallas_call(update_kernel,grid=(cols_//CW,),
        out_shape=jax.ShapeDtypeStruct(mat.shape,BF),
        in_specs=[pl.BlockSpec((rows_,CW),lambda t:(0,t)),vm,pl.BlockSpec((2,NB,CW),lambda t:(0,0,t)),vm,vm],
        out_specs=pl.BlockSpec((rows_,CW),lambda t:(0,t)),
        compiler_params=pltpu.CompilerParams(vmem_limit_bytes=40*2**20))(mat,L,T,pk0,pk1)

def on_device(mat):
    return update(mat,*front(mat))

def solution(mesh):
    return jax.shard_map(on_device,mesh=mesh,in_specs=(P("row","col"),),out_specs=P("row","col"),check_vma=False)
```

time: 109 us -> 83 us (0.76)
  the two profiles are of different devices: /device:TPU:2 before, /device:TPU:4 now
where the time goes in v2:
time: 83 us; the launch traced here: 82.7 us
  Pallas kernels  82.6 us (100%)
    pallas_call x1, Pallas kernels, front(): pl.pallas_call(front_kernel, out_shape=[jax.ShapeDtypeStruct((2, rows_, N...  68.6 us
    pallas_call x1, Pallas kernels, update(): pl.pallas_call(update_kernel, grid=(cols_ // CW,), out_shape=jax.ShapeDty...  14 us

profile of v2, /device:TPU:4, one launch (start us, length us, event | category | flops | bytes accessed | tf_op | source)
XLA Modules:
  0.0 82.7 jit_solution(5350998117244090789)
XLA Ops:
  0.0 68.6 %shard_map.17 = (bf16[2,1792,256]{2,1,0:T(8,128)(2,1)S(1)}, bf16[2,256,3584]{2,1,0:T(8,128)(2,1)S(1)}, bf16[256,256]{1,0:T(8,128)(2,1)S(1)}, bf16[256,256]{1,0:T(8,128)(2,1)S(1)}) custom-call(bf16[1792,3584]{1,0:T(8,128)(2,1)} %a.1), custom_call_target="tpu_custom_call" | custom-call | tf_op jit(solution)/shard_map/pallas_call | solution.py:329
  68.6 14.0 %shard_map.18 = bf16[1792,3584]{1,0:T(8,128)(2,1)} custom-call(bf16[1792,3584]{1,0:T(8,128)(2,1)} %a.1, bf16[2,1792,256]{2,1,0:T(8,128)(2,1)S(1)} %get-tuple-element.9.L, bf16[2,256,3584]{2,1,0:T(8,128)(2,1)S(1)} %get-tuple-element.10.T, bf16[256,256]{1,0:T(8,128)(2,1)S(1)} %get-tuple-element.11.pk0, bf16[256,256]{1,0:T(8,128)(2,1)S(1)} %get-tuple-element.12.pk1), custom_call_target="tpu_custom_call" | custom-call | tf_op jit(solution)/shard_map/pallas_call | solution.py:367

commit v3 on v2

--- a/solution.py
+++ b/solution.py
@@ -113,35 +113,35 @@
 NY=4
 CP=NB//NC
 MESH=pl.DeviceIdType.MESH
-AT=dict(d3=(1,),lg=(2,),s2=(3,1),g1=(6,4),g2=(8,6))
+AT=dict(d3=(1,),lg=(4,),s2=(3,1),g1=(6,4),g2=(8,6),g3=(13,11))
 
 def front_kernel(mat, Lout, Tout, pk0, pk1,
                  Lraw, Traw, li0, ut0, li1, ut1, l10, t01, corner, W, V, U, LT, LI, UT,
                  p1s, p1r, p2s, p2r, c3s, c3r, d3s, d3r, lss, lsr, lgs, lgr,
-                 s1s, s1r, s2s, s2p, s2r, g1s, g1r, g2s, g2r, loc):
+                 s1s, s1r, s2s, s2p, s2r, g1s, g1r, g2s, g2r, g3s, g3r, loc):
     row=lax.axis_index("row"); col=lax.axis_index("col")
-    y=lax.rem(row,NY); z=row//NY
+    y=jnp.bitwise_and(row,NY-1); z=jnp.right_shift(row,2)
     cols=mat.shape[1]
     PL=mat.shape[0]//NC
     H=cols//2
 
-    def rp_(j): return lax.rem(row+j,NR)
-    def cp_(j): return lax.rem(col+j,NC)
+    def rp_(j): return jnp.bitwise_and(row+j,NR-1)
+    def cp_(j): return jnp.bitwise_and(col+j,NC-1)
     def rows(k,n): return pl.ds(pl.multiple_of(k*n,n),n)
     def rc(src,dst,ss,rs,**dev):
-        return pltpu.make_async_remote_copy(src_ref=src,dst_ref=dst,send_sem=ss,recv_sem=rs,device_id=dev,device_id_type=MESH)
+        to=(dev.get("row",row),dev.get("col",col))
+        return pltpu.make_async_remote_copy(src_ref=src,dst_ref=dst,send_sem=ss,recv_sem=rs,device_id=to,device_id_type=MESH)
+    def took(ref,sem): pltpu.make_async_copy(ref,ref,sem).wait()
     def loop(n,f):
-        def b(j,_):
-            f(j); return 0
-        lax.fori_loop(1,n,b,0)
+        for j in range(1,n): f(j)
 
     bar=pltpu.get_barrier_semaphore()
-    loop(NR,lambda j: pl.semaphore_signal(bar,inc=1,device_id={"row":rp_(j)},device_id_type=MESH))
-    loop(NC,lambda j: pl.semaphore_signal(bar,inc=1,device_id={"col":cp_(j)},device_id_type=MESH))
+    loop(NR,lambda j: pl.semaphore_signal(bar,inc=1,device_id=(rp_(j),col),device_id_type=MESH))
+    loop(NC,lambda j: pl.semaphore_signal(bar,inc=1,device_id=(row,cp_(j)),device_id_type=MESH))
     pl.semaphore_wait(bar,NR-1+NC-1)
 
     Q=NB//NY; PC=Q//NY
-    def nx(v,d): return lax.rem(v+d,NY)
+    def nx(v,d): return jnp.bitwise_and(v+d,NY-1)
     def half(h): return slice(0,H) if h==0 else slice(H,2*H)
     def ab(h): return (z,y) if h==0 else (y,z)
     def dev(h,a,b): return a*NY+b if h==0 else b*NY+a
@@ -149,7 +149,7 @@
     def tq(i,h,a): return Traw.at[i,rows(a,Q),half(h)]
     def s1(i,h,d):
         a,b=ab(h); a2=nx(a,d)
-        return rc(qref(mat,h,a2),tq(i,h,a2),s1s.at[h,d],s1r.at[i,h],row=dev(h,a2,b))
+        return rc(qref(mat,h,a2),tq(i,h,a2),s1s.at[h],s1r.at[i,h],row=dev(h,a2,b))
     def s1l(i,h):
         a,b=ab(h); return pltpu.make_async_copy(qref(mat,h,a),tq(i,h,a),loc.at[1+h])
     def scatter(i):
@@ -158,7 +158,7 @@
             for h in range(2):
                 s1l(i,h).start(); loop(NY,lambda d: s1(i,h,d).start())
     def p1(b,j):
-        c=cp_(j); return rc(mat.at[rows(c,CP),0:NB],corner.at[b,rows(c,CP)],p1s.at[j],p1r.at[b%2],col=c)
+        c=cp_(j); return rc(mat.at[rows(c,CP),0:NB],corner.at[b,rows(c,CP)],p1s.at[0],p1r.at[b%2],col=c)
     def p1w(b):
         pl.when(col!=b%2)(lambda: p1(b,1).wait_recv())
     for i in range(2):
@@ -173,13 +173,12 @@
     mine=rows(col,CP)
     def p2(n,j):
         r=(corner.at[0,mine],corner.at[1,mine],corner.at[2:4,mine])[n]
-        return rc(r,r,p2s.at[n,j],p2r.at[n],row=rp_(j))
-    def c3(j): return rc(corner.at[0,mine],corner.at[0,mine],c3s.at[j],c3r.at[col],col=cp_(j))
-    def d3(j): return rc(corner.at[1:4,mine],corner.at[1:4,mine],d3s.at[j],d3r.at[col],col=cp_(j))
-    def c3w(j):
-        c=cp_(j); rc(corner.at[0,rows(c,CP)],corner.at[0,rows(c,CP)],c3s.at[j],c3r.at[c],col=c).wait_recv()
-    def d3w(j):
-        c=cp_(j); rc(corner.at[1:4,rows(c,CP)],corner.at[1:4,rows(c,CP)],d3s.at[j],d3r.at[c],col=c).wait_recv()
+        return rc(r,r,p2s.at[n],p2r.at[n],row=rp_(j))
+    def c3(j): return rc(corner.at[0,mine],corner.at[0,mine],c3s.at[0],c3r.at[0],col=cp_(j))
+    def d3(j): return rc(corner.at[1:4,mine],corner.at[1:4,mine],d3s.at[0],d3r.at[0],col=cp_(j))
+    G=(NC-1)*CP
+    def c3w(): took(corner.at[0,0:G],c3r.at[0])
+    def d3w(): took(corner.at[1:4,0:G],d3r.at[0])
     @pl.when(row==0)
     def _():
         p1w(0); loop(NR,lambda j: p2(0,j).start())
@@ -188,12 +187,12 @@
     loop(NC,lambda j: c3(j).start())
 
     def ls(i,j):
-        k=cp_(j); return rc(mat.at[rows(k,PL),0:NB],Lraw.at[i,rows(k,PL)],lss.at[j],lsr.at[i],col=k)
+        k=cp_(j); return rc(mat.at[rows(k,PL),0:NB],Lraw.at[i,rows(k,PL)],lss.at[0],lsr.at[i],col=k)
     def ll(i): return pltpu.make_async_copy(mat.at[rows(col,PL),0:NB],Lraw.at[i,rows(col,PL)],loc.at[3])
     def lg(i,j):
-        k=cp_(j); return rc(Lraw.at[i,rows(col,PL)],Lraw.at[i,rows(col,PL)],lgs.at[i,j],lgr.at[i,col],col=k)
-    def lgw(i,j):
-        k=cp_(j); rc(Lraw.at[i,rows(k,PL)],Lraw.at[i,rows(k,PL)],lgs.at[i,j],lgr.at[i,k],col=k).wait_recv()
+        k=cp_(j); return rc(Lraw.at[i,rows(col,PL)],Lraw.at[i,rows(col,PL)],lgs.at[i],lgr.at[i],col=k)
+    GL=(NC-1)*PL
+    def lgw(i): took(Lraw.at[i,0:GL],lgr.at[i])
     def left_gather():
         for i in range(2):
             pl.when(col==i)(lambda: ll(i).wait())
@@ -204,19 +203,19 @@
     def tp(i,h,a,b): return Traw.at[i,rows(a*NY+b,PC),half(h)]
     def s2(i,h,d):
         a,b=ab(h); b2=nx(b,d)
-        return rc(tp(i,h,a,b2),tp(i,h,a,b2),s2s.at[i,h,d],s2r.at[i,h],row=dev(h,a,b2))
+        return rc(tp(i,h,a,b2),tp(i,h,a,b2),s2s.at[i,h],s2r.at[i,h],row=dev(h,a,b2))
     def g1(i,h,d,ss):
         a,b=ab(h); b2=nx(b,d)
-        return rc(tp(i,h,a,b),tp(i,h,a,b),ss.at[i,h,d],g1r.at[i,h,b],row=dev(h,a,b2))
-    def g1w(i,h,d):
-        a,b=ab(h); b2=nx(b,d)
-        rc(tp(i,h,a,b2),tp(i,h,a,b2),g1s.at[i,h,d],g1r.at[i,h,b2],row=dev(h,a,b2)).wait_recv()
+        return rc(tp(i,h,a,b),tp(i,h,a,b),ss.at[i,h],g1r.at[i,h],row=dev(h,a,b2))
+    def tt(i,h,n): return Traw.at[i,0:n,half(h)]
+    def g1w(i,h): took(tt(i,h,3*PC),g1r.at[i,h])
     def g2(i,h,d):
-        a,b=ab(h); a2=nx(a,d)
-        return rc(tq(i,h,a),tq(i,h,a),g2s.at[i,h,d],g2r.at[i,h,a],row=dev(h,a2,b))
-    def g2w(i,h,d):
-        a,b=ab(h); a2=nx(a,d)
-        rc(tq(i,h,a2),tq(i,h,a2),g2s.at[i,h,d],g2r.at[i,h,a2],row=dev(h,a2,b)).wait_recv()
+        a,b=ab(h)
+        return rc(tq(i,h,a),tq(i,h,a),g2s.at[i,h],g2r.at[i,h],row=dev(h,nx(a,d),b))
+    def g3(i,h,d):
+        a,b=ab(h); r=Traw.at[i,pl.ds(pl.multiple_of(nx(a,NY-d)*Q+(0 if d==1 else Q//2),Q//2),Q//2),half(h)]
+        return rc(r,r,g3s.at[i,h],g3r.at[i,h],row=dev(h,nx(a,d),b))
+    def g3w(i,h): took(tt(i,h,Q),g3r.at[i,h])
     each=[(i,h) for i in range(2) for h in range(2)]
     def inner_is_src(i,h): return ab(h)[1]==src_ab(h,i)[1]
     def top_s2(n):
@@ -241,8 +240,8 @@
         for i,h in each:
             if i!=n: continue
             @pl.when(ab(h)[1]!=src_ab(h,i)[1])
-            def _(i=i,h=h): loop(NY,lambda d: g1w(i,h,d))
-            loop(NY,lambda d: g2(i,h,d).start())
+            def _(i=i,h=h): g1w(i,h)
+            for d in (1,NY-1): g2(i,h,d).start()
 
     for i in range(2):
         if i==0: scatter(0)
@@ -255,7 +254,7 @@
     @pl.when(row==1)
     def _():
         p1w(2); p1w(3); loop(NR,lambda j: p2(2,j).start())
-    loop(NC,c3w)
+    c3w()
     def rest_corners():
         pl.when(row!=0)(lambda: p2(1,1).wait_recv())
         pl.when(row!=1)(lambda: p2(2,1).wait_recv())
@@ -264,20 +263,41 @@
     def dump(li,ut):
         for ref,src in ((li,LI),(ut,UT)):
             for n,x in enumerate(split2(src[...])): ref[n]=x
+    def top_g3(n):
+        for h in range(2):
+            took(tt(n,h,2*Q),g2r.at[n,h])
+            for d in (1,NY-1): g3(n,h,d).start()
+    def drain():
+        for i in range(2):
+            pl.when((row==i)&(col<2))(lambda: took(corner.at[0,0:G],p1s.at[0]))
+            pl.when(col==i)(lambda: took(Lraw.at[0,0:GL],lss.at[0]))
+        @pl.when(row==0)
+        def _():
+            for n in range(2): took(Lraw.at[0,0:(NR-1)*CP],p2s.at[n])
+        pl.when(row==1)(lambda: took(Lraw.at[0,0:2*(NR-1)*CP],p2s.at[2]))
+        took(corner.at[0,0:G],c3s.at[0]); took(corner.at[1:4,0:G],d3s.at[0])
+        for i,h in each:
+            b=ab(h)[1]; sb=src_ab(h,i)[1]
+            pl.when(row==i)(lambda: took(tt(0,h,3*Q),s1s.at[h]))
+            @pl.when(b==sb)
+            def _(i=i,h=h):
+                took(tt(0,h,3*PC),s2s.at[i,h]); took(tt(0,h,3*PC),s2p.at[i,h])
+            pl.when(b!=sb)(lambda: took(tt(0,h,2*PC),g1s.at[i,h]))
     acts=[(AT["d3"][0],rest_corners),(AT["lg"][0],left_gather)]
-    for f,n in ((top_s2,"s2"),(top_g1,"g1"),(top_g2,"g2")):
+    for f,n in ((top_s2,"s2"),(top_g1,"g1"),(top_g2,"g2"),(top_g3,"g3")):
         acts+=[(AT[n][k],functools.partial(f,k)) for k in (0,1)]
     lu_inv(corner[0],W,V,U,LT,LI,UT,[x for x in acts if x[0]<8])
     finish(U,LT,pk0); dump(li0,ut0)
-    loop(NC,d3w)
+    d3w()
     L=sum(dotT(corner[2],ut0[n]) for n in (1,0)).astype(BF)
     T=sum(jnp.dot(li0[n],corner[1],preferred_element_type=F) for n in (1,0)).astype(BF)
     l10[...]=L; t01[...]=T
     a=(corner[3].astype(F)-jnp.dot(L,T,preferred_element_type=F)).astype(BF)
     lu_inv(a,W,V,U,LT,LI,UT,[(x[0]-8,x[1]) for x in acts if x[0]>=8])
     finish(U,LT,pk1); dump(li1,ut1)
+    drain()
     for i in range(2):
-        loop(NC,lambda j: lgw(i,j))
+        lgw(i)
     def mm(x,y): return jnp.dot(x,y,preferred_element_type=F)
     LB=NB
     def lsolve(k,_):
@@ -288,38 +308,27 @@
         x=(Lraw[1,w].astype(F)-mm(x,t01[...])).astype(BF)
         Lout[1,w]=(dotT(x,ut1[1])+dotT(x,ut1[0])).astype(BF)
         return 0
-    lax.fori_loop(0,mat.shape[0]//LB,lsolve,0)
+    lax.fori_loop(0,mat.shape[0]//LB,lsolve,0,unroll=True)
     TB=cols//7
     for i,h in each:
-        if i==0: loop(NY,lambda d: g2w(i,h,d))
+        if i==0: g3w(i,h)
     def tsolve0(k,_):
         w=pl.ds(pl.multiple_of(k*TB,TB),TB)
         x=Traw[0,:,w]
         Tout[0,:,w]=(mm(li0[1],x)+mm(li0[0],x)).astype(BF)
         return 0
-    lax.fori_loop(0,7,tsolve0,0)
+    lax.fori_loop(0,7,tsolve0,0,unroll=True)
     for i,h in each:
-        if i==1: loop(NY,lambda d: g2w(i,h,d))
+        if i==1: g3w(i,h)
     def tsolve1(k,_):
         w=pl.ds(pl.multiple_of(k*TB,TB),TB)
         x=(Traw[1,:,w].astype(F)-mm(l10[...],Tout[0,:,w])).astype(BF)
         Tout[1,:,w]=(mm(li1[1],x)+mm(li1[0],x)).astype(BF)
         return 0
-    lax.fori_loop(0,7,tsolve1,0)
-    for i in range(2):
-        for jj in range(2):
-            pl.when((row==i)&(col==jj))(lambda: loop(NC,lambda j: p1(2*i+jj,j).wait_send()))
-        pl.when(col==i)(lambda: loop(NC,lambda j: ls(i,j).wait_send()))
-        loop(NC,lambda j: lg(i,j).wait_send())
-    pl.when(row==0)(lambda: loop(NR,lambda j: (p2(0,j).wait_send(),p2(1,j).wait_send())))
-    pl.when(row==1)(lambda: loop(NR,lambda j: p2(2,j).wait_send()))
-    loop(NC,lambda j: (c3(j).wait_send(),d3(j).wait_send()))
+    lax.fori_loop(0,7,tsolve1,0,unroll=True)
+    for i in range(2): took(Lraw.at[i,0:GL],lgs.at[i])
     for i,h in each:
-        b=ab(h)[1]; sb=src_ab(h,i)[1]
-        pl.when(row==i)(lambda: loop(NY,lambda d: s1(i,h,d).wait_send()))
-        pl.when(b==sb)(lambda: loop(NY,lambda d: (s2(i,h,d).wait_send(),g1(i,h,d,s2p).wait_send())))
-        pl.when(b!=sb)(lambda: loop(NY,lambda d: pl.when(nx(b,d)!=sb)(lambda: g1(i,h,d,g1s).wait_send())))
-        loop(NY,lambda d: g2(i,h,d).wait_send())
+        took(tt(i,h,2*Q),g2s.at[i,h]); took(tt(i,h,Q),g3s.at[i,h])
 
 def front(mat):
     rows_,cols_=mat.shape
@@ -330,9 +339,9 @@
         out_shape=[jax.ShapeDtypeStruct((2,rows_,NB),BF),jax.ShapeDtypeStruct((2,NB,cols_),BF),s,s],
         in_specs=[an],out_specs=[vm]*4,
         scratch_shapes=[pltpu.VMEM((2,rows_,NB),BF),pltpu.VMEM((2,NB,cols_),BF)]+[pltpu.VMEM((2,NB,NB),BF)]*4+[pltpu.VMEM((NB,NB),BF)]*2+[pltpu.VMEM((4,NB,NB),BF)]+[pltpu.VMEM((NB,NB),F)]*6+[
-            dma((NC,)),dma((2,)),dma((3,NR)),dma((3,)),dma((NC,)),dma((NC,)),dma((NC,)),dma((NC,)),
-            dma((NC,)),dma((2,)),dma((2,NC)),dma((2,NC)),
-            dma((2,NY)),dma((2,2)),dma((2,2,NY)),dma((2,2,NY)),dma((2,2)),dma((2,2,NY)),dma((2,2,NY)),dma((2,2,NY)),dma((2,2,NY)),dma((4,))],
+            dma((1,)),dma((2,)),dma((3,)),dma((3,)),dma((1,)),dma((1,)),dma((1,)),dma((1,)),
+            dma((1,)),dma((2,)),dma((2,)),dma((2,)),
+            dma((2,)),dma((2,2)),dma((2,2)),dma((2,2)),dma((2,2)),dma((2,2)),dma((2,2)),dma((2,2)),dma((2,2)),dma((2,2)),dma((2,2)),dma((4,))],
         compiler_params=pltpu.CompilerParams(collective_id=0,has_side_effects=True,vmem_limit_bytes=40*2**20))(mat)
 
 def update_kernel(a, L, T, pk0, pk1, out):

time: 83 us -> 74.8 us (0.901)
  Pallas kernels: 82.6 us -> 74.5 us
    pallas_call x1, Pallas kernels: 68.6 us -> 60.4 us  [front(): pl.pallas_call(front_kernel, out_shape=[jax.ShapeDtypeStruct((2, rows_, N...]
where the time goes in v3:
time: 74.8 us; the launch traced here: 74.5 us
  Pallas kernels  74.5 us (100%)
    pallas_call x1, Pallas kernels, front(): pl.pallas_call(front_kernel, out_shape=[jax.ShapeDtypeStruct((2, rows_, N...  60.4 us
    pallas_call x1, Pallas kernels, update(): pl.pallas_call(update_kernel, grid=(cols_ // CW,), out_shape=jax.ShapeDty...  14 us

profile of v3, /device:TPU:4, one launch (start us, length us, event | category | flops | bytes accessed | tf_op | source)
XLA Modules:
  0.0 74.5 jit_solution(10090895907603306064)
XLA Ops:
  0.0 60.4 %shard_map.17 = (bf16[2,1792,256]{2,1,0:T(8,128)(2,1)S(1)}, bf16[2,256,3584]{2,1,0:T(8,128)(2,1)S(1)}, bf16[256,256]{1,0:T(8,128)(2,1)S(1)}, bf16[256,256]{1,0:T(8,128)(2,1)S(1)}) custom-call(bf16[1792,3584]{1,0:T(8,128)(2,1)} %a.1), custom_call_target="tpu_custom_call" | custom-call | tf_op jit(solution)/shard_map/pallas_call | solution.py:338
  60.5 14.0 %shard_map.18 = bf16[1792,3584]{1,0:T(8,128)(2,1)} custom-call(bf16[1792,3584]{1,0:T(8,128)(2,1)} %a.1, bf16[2,1792,256]{2,1,0:T(8,128)(2,1)S(1)} %get-tuple-element.9.L, bf16[2,256,3584]{2,1,0:T(8,128)(2,1)S(1)} %get-tuple-element.10.T, bf16[256,256]{1,0:T(8,128)(2,1)S(1)} %get-tuple-element.11.pk0, bf16[256,256]{1,0:T(8,128)(2,1)S(1)} %get-tuple-element.12.pk1), custom_call_target="tpu_custom_call" | custom-call | tf_op jit(solution)/shard_map/pallas_call | solution.py:376
